TPU v7x, 128 devices: a whole 4x4x4 slice. The times are simulated.
128 devices in a mesh: lat: 8 (over x, y_lo), lon: 16 (over z, y_hi, core).
Axes of the slice: x: 4, y: 4 (y_hi: 2, y_lo: 2; y = y_hi * 2 + y_lo), z: 4, core: 2. Of those that a mesh axis runs over, the one named last changes fastest.
Arguments:
- tokens: bfloat16 [2, 96, 384, 512], P(None, 'lat', 'lon'), may hold values from -6 to 6
- land_sea: int32 [96, 384], P('lat', 'lon'), may hold values 0 or 1
- land_vec: bfloat16 [512], replicated, may hold values from -4 to 4
- fine_gain: bfloat16 [512], replicated, may hold values from 0.5 to 1.5
- fine_qkv: bfloat16 [512, 1536], replicated, may hold values from -2 to 2
- fine_proj: bfloat16 [512, 512], replicated, may hold values from -0.25 to 0.25
- merge_gain: bfloat16 [2048], replicated, may hold values from 0.5 to 1.5
- merge_weight: bfloat16 [2048, 1024], replicated, may hold values from -0.125 to 0.125
- coarse_gain: bfloat16 [1024], replicated, may hold values from 0.5 to 1.5
- coarse_qkv: bfloat16 [1024, 3072], replicated, may hold values from -2 to 2
- coarse_proj: bfloat16 [1024, 1024], replicated, may hold values from -0.1875 to 0.1875
- cotangent: bfloat16 [2, 48, 192, 1024], P(None, 'lat', 'lon'), may hold values from -6 to 6
Outputs:
- coarse_out: bfloat16 [2, 48, 192, 1024], P(None, 'lat', 'lon')
- grad_tokens: bfloat16 [2, 96, 384, 512], P(None, 'lat', 'lon')
- fine_grads: float32 [512, 2048], P('lat', 'lon')
All inputs are finite; a program needn't handle non-finite values. No bound on the sum of `land_sea` on one device may be relied on, other than what follows from the above.
Results may differ from a plain program's by a relative error of at most 0.03.
Values may be sent and summed in bfloat16 or wider, within the bound.
No kernel may reach another device: no remote copies, remote signals or barrier semaphores. Data moves between devices by JAX's collectives and lax.ppermute only.
A program may use at most 128 MiB of HBM per device.

v0:
```python
import math

import jax
import jax.numpy as jnp
import numpy as np
from jax import lax
from jax.experimental import pallas as pl
from jax.experimental.pallas import tpu as pltpu
from jax.sharding import PartitionSpec as P

F32 = jnp.float32
BF16 = jnp.bfloat16
EPSILON = 1e-05
NEG = -1e30

QUADS = ((0, 0), (1, 0), (0, 1), (1, 1))
SROWS = 400
TAIL = 144
PIECES = ((0, 144), (144, 80), (224, 80), (304, 48))
EXT = 1408
QRY = 768
CRS = 192

E_OFF = {
    0: (0, 576, 896, 1216),
    1: (144, 736, 976, 1312),
    2: (288, 656, 1056, 1264),
    3: (432, 816, 1136, 1360),
}
Q_OFF = {
    0: (0, 192, 384, 576),
    1: (48, 288, 432, 672),
    2: (96, 240, 480, 624),
    3: (144, 336, 528, 720),
}
CORDER = (0, 2, 1, 3)
C_OFF = {quad: 48 * place for place, quad in enumerate(CORDER)}

WINDOWS = (
    (0, 144, 0, 48, 0),
    (144, 144, 48, 48, 0),
    (288, 144, 96, 48, 0),
    (432, 144, 144, 48, 0),
    (576, 160, 192, 96, 1),
    (736, 160, 288, 96, 1),
    (896, 160, 384, 96, 2),
    (1056, 160, 480, 96, 2),
    (1216, 192, 576, 192, 3),
)


def piece_cells(quad):
    qr, qc = QUADS[quad]
    near_r, far_r, mid_r = ((1, 0, 2), (4, 5, 3))[qr]
    near_c, far_c, mid_c = ((1, 0, 2), (4, 5, 3))[qc]
    return (
        ((near_r, near_c), (near_r, far_c), (far_r, near_c), (far_r, far_c)),
        ((near_r, mid_c), (far_r, mid_c)),
        ((mid_r, near_c), (mid_r, far_c)),
        ((mid_r, mid_c),),
    )


def build_tables():
    pick = np.full((8, 384), -1, np.int32)
    cell_query = {}
    for quad in range(4):
        qr, qc = QUADS[quad]
        place = 0
        for cells, q_off in zip(piece_cells(quad), Q_OFF[quad]):
            cell_query[cells[0]] = q_off
            for cr, cc in cells:
                for lev in range(2):
                    for i in range(3):
                        for j in range(6):
                            row = 3 * cr + i + 3 - 12 * qr
                            col = 6 * cc + j + 6 - 24 * qc
                            pick[quad, place] = lev * 288 + row * 24 + col
                            place += 1
    expand = np.full((8, 384), -1, np.int32)
    for start, first, rows in ((0, 0, 72), (80, 72, 72), (160, 144, 36), (208, 184, 36), (256, 220, 36)):
        expand[0, start : start + rows] = first + np.arange(rows)
    cpick = np.full((16, 128), -1, np.int32)
    merge = np.zeros((4, CRS, QRY), np.float32)
    for quad in range(4):
        qr, qc = QUADS[quad]
        for lev in range(2):
            for i in range(3):
                for j in range(6):
                    place = lev * 18 + i * 6 + j
                    row = i + 3 * (1 - qr)
                    col = j + 6 * (1 - qc)
                    spot = (row * 12 + col) * 2 + lev
                    cpick[quad, 72 + place] = spot
                    if place < 20:
                        cpick[4 + quad, 108 + place] = spot
                    else:
                        cpick[8 + quad, place - 20] = spot
                    for k, (di, dj) in enumerate(((0, 0), (1, 0), (0, 1), (1, 1))):
                        er = 3 + 2 * (3 * qr + i) + di
                        ec = 6 + 2 * (6 * qc + j) + dj
                        spot = cell_query[(er // 3, ec // 6)] + lev * 18 + (er % 3) * 6 + ec % 6
                        merge[k, C_OFF[quad] + place, spot] = 1
    return pick, cpick, expand, merge


PICK, CPICK, EXPAND, MERGE = build_tables()


def nn(left, right):
    return jnp.dot(left, right, preferred_element_type=F32)


def nt(left, right):
    return lax.dot_general(left, right, (((1,), (1,)), ((), ())), preferred_element_type=F32)


def tn(left, right):
    return lax.dot_general(left, right, (((0,), (0,)), ((), ())), preferred_element_type=F32)


def column(row):
    return jnp.broadcast_to(row, (128, 128)).T


def one_hot(row, count):
    blocks = []
    col = column(row)
    lane = lax.broadcasted_iota(jnp.int32, (128, 128), 1)
    for start in range(0, count, 128):
        hit = col == lane + start
        blocks.append(jnp.where(hit, 1.0, 0.0).astype(BF16))
    return jnp.concatenate(blocks, axis=1)[:, :count]


def one_hot_back(row, count):
    spot = lax.broadcasted_iota(jnp.int32, (count, row.shape[1]), 0)
    return jnp.where(spot == row, 1.0, 0.0).astype(BF16)


def pull(sources, targets, sems):
    copies = []
    for number, (source, target) in enumerate(zip(sources, targets)):
        copies.append(pltpu.make_async_copy(source, target, sems.at[number]))
        copies[-1].start()
    return copies


def prep_kernel(*refs):
    sources, outs, targets = refs[:6], refs[6:10], refs[10:16]
    tok, land_in, vec_in, cot_in, pick, cpick = targets
    square, stream, built, sems, out_sems = refs[16:]
    copies = pull(sources, targets, sems)
    square[...] = jnp.zeros_like(square)
    for number in (1, 2, 4, 0):
        copies[number].wait()
    square[0:12, 0:24] = land_in[...].astype(F32)
    flags = square[...].T
    vec = vec_in[...].astype(F32).reshape(1, 512)
    for step in range(12):
        row = 2 * step % 12
        land = jnp.concatenate([flags[0:24, row : row + 1], flags[0:24, row + 1 : row + 2]], axis=0)
        spot = slice(48 * step, 48 * step + 48)
        stream[spot, :] = (tok[spot, :].astype(F32) + land * vec).astype(BF16)
    copies[3].wait()
    copies[5].wait()
    cot = cot_in[...].reshape(144, 1024)
    leaving = []
    for quad in (1, 2, 3, 0):
        out = built.at[quad]
        choice = jnp.concatenate(
            [one_hot(pick[quad : quad + 1, n : n + 128], 576) for n in (0, 128, 256)], axis=0
        )
        value = nn(choice, stream[...])
        out[0:256, :] = value[0:256].astype(BF16)
        first = one_hot(cpick[quad : quad + 1, :], 144)
        second = one_hot(cpick[4 + quad : 5 + quad, :], 144)
        value = value[256:384] + nn(first, cot[:, 0:512]) + nn(second, cot[:, 512:1024])
        out[256:384, :] = value.astype(BF16)
        rest = one_hot(cpick[8 + quad : 9 + quad, :], 144)[:16]
        out[384:400, :] = nn(rest, cot[:, 512:1024]).astype(BF16)
        leaving.append(pltpu.make_async_copy(out, outs[quad], out_sems.at[quad]))
        leaving[-1].start()
    for copy in leaving:
        copy.wait()


HBM = pl.BlockSpec(memory_space=pltpu.HBM)
VMEM = pl.BlockSpec(memory_space=pltpu.VMEM)


def prep(tokens, land, vec, cot, pick, cpick):
    operands = (tokens, land, vec, cot, pick, cpick)
    return pl.pallas_call(
        prep_kernel,
        out_shape=(jax.ShapeDtypeStruct((SROWS, 512), BF16),) * 4,
        in_specs=[HBM] * 6,
        out_specs=(HBM,) * 4,
        scratch_shapes=[pltpu.VMEM(value.shape, value.dtype) for value in operands]
        + [
            pltpu.VMEM((128, 128), F32),
            pltpu.VMEM((576, 512), BF16),
            pltpu.VMEM((4, SROWS, 512), BF16),
            pltpu.SemaphoreType.DMA((6,)),
            pltpu.SemaphoreType.DMA((4,)),
        ],
        compiler_params=pltpu.CompilerParams(vmem_limit_bytes=60 * 2**20),
    )(*operands)


def finish_kernel(*refs):
    sources, grad_ref, coarse_ref, targets, sems = refs[:6], refs[6], refs[7], refs[8:14], refs[14]
    pick, cpick = targets[:2]
    copies = pull(sources, targets, sems)
    copies[0].wait()
    copies[1].wait()
    choices, firsts, seconds, rests = [], [], [], []
    for quad in range(4):
        choices.append(one_hot_back(pick[quad : quad + 1, :], 576))
        firsts.append(one_hot_back(cpick[quad : quad + 1, :], 144))
        seconds.append(one_hot_back(cpick[4 + quad : 5 + quad, :], 144))
        rests.append(one_hot_back(cpick[8 + quad : 9 + quad, :], 144)[:, :16])
    for copy in copies[2:]:
        copy.wait()

    def joined(low, high):
        return jnp.concatenate([ref[low:high, :] for ref in targets[2:]], axis=0)

    total = nn(jnp.concatenate(choices, axis=1), joined(0, 384))
    middle = joined(256, 384)
    left = nn(jnp.concatenate(firsts, axis=1), middle)
    right = nn(jnp.concatenate(seconds, axis=1), middle)
    for quad, ref in enumerate(targets[2:]):
        right = right + nn(rests[quad], ref[384:400, :])
    crs = jnp.concatenate([left, right], axis=1)
    grad_ref[...] = total.astype(BF16)
    coarse_ref[...] = crs.astype(BF16).reshape(72, 2, 1024)


def finish(*operands):
    return pl.pallas_call(
        finish_kernel,
        out_shape=(
            jax.ShapeDtypeStruct((576, 512), BF16),
            jax.ShapeDtypeStruct((72, 2, 1024), BF16),
        ),
        in_specs=[HBM] * 6,
        scratch_shapes=[pltpu.VMEM(value.shape, value.dtype) for value in operands]
        + [pltpu.SemaphoreType.DMA((6,))],
        compiler_params=pltpu.CompilerParams(vmem_limit_bytes=60 * 2**20),
    )(*operands)


def norm_rows(values, gain):
    wide = values.astype(F32)
    centre = jnp.mean(wide, axis=-1, keepdims=True)
    moved = wide - centre
    scale = lax.rsqrt(jnp.mean(moved * moved, axis=-1, keepdims=True) + EPSILON)
    return (moved * scale * gain).astype(BF16), centre, scale


def norm_back(values, gain, centre, scale, d_normed):
    hat = (values.astype(F32) - centre) * scale
    weighted = d_normed * gain
    first = jnp.mean(weighted, axis=-1, keepdims=True)
    second = jnp.mean(weighted * hat, axis=-1, keepdims=True)
    return scale * (weighted - first - hat * second)


def norm_back_fresh(values, gain, d_normed):
    wide = values.astype(F32)
    moved = wide - jnp.mean(wide, axis=-1, keepdims=True)
    scale = lax.rsqrt(jnp.mean(moved * moved, axis=-1, keepdims=True) + EPSILON)
    hat = moved * scale
    weighted = d_normed * gain
    first = jnp.mean(weighted, axis=-1, keepdims=True)
    second = jnp.mean(weighted * hat, axis=-1, keepdims=True)
    return scale * (weighted - first - hat * second)


def lane_masks(rows):
    lane = lax.broadcasted_iota(jnp.int32, (rows, 128), 1)
    return lane < 64


def stacked(values):
    low = lane_masks(values.shape[0])
    zero = jnp.zeros_like(values)
    return jnp.concatenate([jnp.where(low, values, zero), jnp.where(low, zero, values)], axis=0)


def unstacked(values):
    half = values.shape[0] // 2
    return jnp.where(lane_masks(half), values[:half], values[half:])


def attend_all(queries, keys, vals, biases):
    scores = [nt(stacked(query), key) for query, key in zip(queries, keys)]
    scores = [s if bias is None else s + bias for s, bias in zip(scores, biases)]
    tops = [jnp.max(s, axis=-1, keepdims=True) for s in scores]
    raised = [jnp.exp(s - top).astype(BF16) for s, top in zip(scores, tops)]
    wide = [nn(r, jnp.concatenate([v, jnp.ones_like(v)], axis=1)) for r, v in zip(raised, vals)]
    inverse = [1.0 / w[:, 128:] for w in wide]
    mixed = [unstacked(w[:, :128] * i).astype(BF16) for w, i in zip(wide, inverse)]
    return raised, inverse, mixed


def back_all(queries, keys, vals, raised, inverse, mixed, d_mixed):
    d_scaled = [stacked(d).astype(F32) * i for d, i in zip(d_mixed, inverse)]
    twice = [jnp.concatenate([m, m], axis=0).astype(F32) for m in mixed]
    delta = [jnp.sum(d * t, axis=-1, keepdims=True) for d, t in zip(d_scaled, twice)]
    d_short = [d.astype(BF16) for d in d_scaled]
    d_probs = [nt(d, v) for d, v in zip(d_short, vals)]
    d_vals = [tn(r, d).astype(BF16) for r, d in zip(raised, d_short)]
    d_scores = [(r.astype(F32) * (p - t)).astype(BF16) for r, p, t in zip(raised, d_probs, delta)]
    d_query = [(unstacked(nn(d, k)) * 0.125).astype(BF16) for d, k in zip(d_scores, keys)]
    d_keys = [tn(d, stacked(q)).astype(BF16) for d, q in zip(d_scores, queries)]
    return d_query, d_keys, d_vals


def pair_slice(start, pair):
    return pl.ds(pl.multiple_of(start + pair * 128, 128), 128)


def main_kernel(
    q0_ref,
    q1_ref,
    q2_ref,
    q3_ref,
    fgain_ref,
    mgain_ref,
    cgain_ref,
    fqkv_hbm,
    fproj_hbm,
    merge_hbm,
    merge_t_hbm,
    mw_hbm,
    cqkv_hbm,
    cproj_hbm,
    expand_hbm,
    keep_hbm,
    send_hbm,
    dqkv_hbm,
    dmid_hbm,
    cback_hbm,
    x_hbm,
    tails,
    expand,
    x,
    cot,
    fqkv,
    fproj,
    mrg,
    mrg_t,
    mw,
    cqkv,
    cproj,
    sems,
    normed,
    normed_t,
    kv,
    qry,
    att,
    att_t,
    raised_a,
    raised_b,
    raised_c,
    inverse,
    bias_b,
    bias_c,
    mid,
    merged,
    mstat,
    mnormed,
    c_in,
    cstat,
    cnormed,
    cq,
    catt,
    craised,
    cinverse,
    dmid,
    datt,
    dqkv,
    cdnorm,
    cback,
    keep,
    send,
    out_sems,
):
    last = jnp.where(lax.axis_index("lat") == lax.axis_size("lat") - 1, 1, 0)
    core = lax.axis_index("lon") % 2
    leaving = []

    def leave(src, dst):
        copy = pltpu.make_async_copy(src, dst, out_sems.at[len(leaving)])
        copy.start()
        leaving.append(copy)

    weights = (
        (fqkv_hbm, fqkv),
        (fproj_hbm, fproj),
        (merge_hbm, mrg),
        (mw_hbm, mw),
        (cqkv_hbm, cqkv),
        (cproj_hbm, cproj),
        (merge_t_hbm, mrg_t),
    )
    loads = [pltpu.make_async_copy(src, dst, sems.at[n]) for n, (src, dst) in enumerate(weights)]
    pulls = []
    number = len(loads)
    for quad, ref in enumerate((q0_ref, q1_ref, q2_ref, q3_ref)):
        pulls.append(
            pltpu.make_async_copy(
                ref.at[pl.ds(0, TAIL)], x.at[pl.ds(E_OFF[quad][0], TAIL)], sems.at[number]
            )
        )
        pulls.append(
            pltpu.make_async_copy(
                ref.at[pl.ds(TAIL, SROWS - TAIL)], tails.at[quad], sems.at[number + 1]
            )
        )
        number += 2
    pulls.append(pltpu.make_async_copy(expand_hbm, expand, sems.at[number]))
    for copy in pulls:
        copy.start()
    for copy in loads:
        copy.start()

    def bias_of(shape, q_rows, piece, valid, q_half, k_half, split):
        q_at = lax.broadcasted_iota(jnp.int32, shape, 0) % q_rows
        k_at = lax.broadcasted_iota(jnp.int32, shape, 1)
        bad = (k_at % piece) >= valid
        if split:
            other = (q_at >= q_half) != (k_at >= k_half)
            bad = jnp.logical_or(bad, jnp.logical_and(other, last == 1))
        return jnp.where(bad, NEG, 0.0)

    bias_b[0] = bias_of((192, 160), 96, 80, 72, 48, 80, False)
    bias_b[1] = bias_of((192, 160), 96, 80, 72, 48, 80, True)
    bias_c[...] = bias_of((384, 192), 192, 48, 36, 96, 96, True)

    spread_out = []
    for copy in pulls:
        copy.wait()
    for start in (0, 128, 256):
        spread_out.append(one_hot(expand[0:1, start : start + 128], 256))
    spread_out = jnp.concatenate(spread_out, axis=0)[:304]
    for quad in range(4):
        value = nn(spread_out, tails[quad]).astype(BF16)
        for (start, rows), off in list(zip(PIECES, E_OFF[quad]))[1:]:
            x[pl.ds(off, rows), :] = value[start - TAIL : start - TAIL + rows]
        for half in range(2):
            cot[half, pl.ds(C_OFF[quad], 48), :] = value[208 + 48 * half : 256 + 48 * half]
    leave(x, x_hbm)
    fgain = fgain_ref[...].astype(F32)

    for step in range(11):
        rows = pl.ds(step * 128, 128)
        result, _, _ = norm_rows(x[rows, :], fgain)
        normed[rows, :] = result
        normed_t[:, rows] = result.T

    def cells(read):
        parts = []
        for q_start in range(0, QRY, 48):
            for quad in range(4):
                for e_off, q_off in zip(E_OFF[quad], Q_OFF[quad]):
                    if q_off == q_start:
                        parts.append(read(e_off))
        return jnp.concatenate(parts, axis=0)

    loads[0].wait()

    for step in range(4):
        kv[:, pl.ds(step * 256, 256)] = nn(
            normed[...], fqkv[:, pl.ds(512 + step * 256, 256)]
        ).astype(BF16)

    @pl.loop(0, 2)
    def _(step):
        cols = pl.ds(pl.multiple_of(step * 256, 256), 256)
        left = cells(lambda off: normed[pl.ds(off, 48), :])
        qry[:, cols] = (nn(left, fqkv[:, cols]).astype(BF16) * 0.125).astype(BF16)

    def raised_at(index, pair):
        kind = WINDOWS[index][4]
        if kind == 0:
            return raised_a.at[pair, index]
        if kind == 3:
            return raised_c.at[pair]
        return raised_b.at[pair, index - 4]

    def bias_at(kind):
        if kind == 0:
            return None
        return bias_c[...] if kind == 3 else bias_b[kind - 1]

    def queries_of(ref, pair):
        return [ref[pl.ds(q_off, q_rows), pair_slice(0, pair)] for _, _, q_off, q_rows, _ in WINDOWS]

    def keys_of(start, pair):
        return [kv[pl.ds(e_off, rows), pair_slice(start, pair)] for e_off, rows, _, _, _ in WINDOWS]

    @pl.loop(0, 4)
    def _(pair):
        raised, inv, mixed = attend_all(
            queries_of(qry, pair),
            keys_of(0, pair),
            keys_of(512, pair),
            [bias_at(window[4]) for window in WINDOWS],
        )
        for index, (_, _, q_off, q_rows, _) in enumerate(WINDOWS):
            raised_at(index, pair)[...] = raised[index]
            inverse[pair, pl.ds(2 * q_off, 2 * q_rows), :] = inv[index]
            att[pl.ds(q_off, q_rows), pair_slice(0, pair)] = mixed[index]

    loads[1].wait()

    @pl.loop(0, 2)
    def _(step):
        cols = pl.ds(pl.multiple_of(step * 256, 256), 256)
        left = cells(lambda off: x[pl.ds(off, 48), cols])
        mid[:, cols] = (left.astype(F32) + nn(att[...], fproj[:, cols])).astype(BF16)

    loads[2].wait()
    for k in range(4):
        merged[:, 512 * k : 512 * k + 512] = nn(mrg[k], mid[...]).astype(BF16)
    mgain = mgain_ref[...].astype(F32)
    result, centre, scale = norm_rows(merged[...], mgain)
    mnormed[...] = result
    mstat[0] = jnp.broadcast_to(centre, (CRS, 128))
    mstat[1] = jnp.broadcast_to(scale, (CRS, 128))
    loads[3].wait()

    for step in range(4):
        cols = pl.ds(step * 256, 256)
        c_in[:, cols] = nn(mnormed[...], mw[:, cols]).astype(BF16)

    cgain = cgain_ref[...].astype(F32)
    result, centre, scale = norm_rows(c_in[...], cgain)
    cnormed[...] = result
    cstat[0] = jnp.broadcast_to(centre, (CRS, 128))
    cstat[1] = jnp.broadcast_to(scale, (CRS, 128))
    loads[4].wait()

    for step in range(6):
        cols = pl.ds(step * 512, 512)
        value = nn(cnormed[...], cqkv[:, cols]).astype(BF16)
        cq[:, cols] = (value * 0.125).astype(BF16) if step < 2 else value

    def coarse_of(ref, start, group):
        return [ref[:, pair_slice(start, 4 * group + n)] for n in range(4)]

    @pl.loop(0, 2)
    def _(group):
        raised, inv, mixed = attend_all(
            coarse_of(cq, 0, group),
            coarse_of(cq, 1024, group),
            coarse_of(cq, 2048, group),
            [bias_c[...]] * 4,
        )
        for n in range(4):
            craised[4 * group + n] = raised[n]
            cinverse[4 * group + n] = inv[n]
            catt[:, pair_slice(0, 4 * group + n)] = mixed[n]

    loads[5].wait()
    for half in range(2):
        cols = slice(512 * half, 512 * half + 512)
        c_mid = (c_in[:, cols].astype(F32) + nn(catt[...], cproj[:, cols])).astype(BF16)
        for quad in range(4):
            off = C_OFF[quad]
            cback[quad, 48 * half : 48 * half + 48, :] = c_mid[off : off + 48]

    leave(cback, cback_hbm)

    dcot = jnp.concatenate([cot[0], cot[1]], axis=1)
    dcatt = nt(dcot, cproj[...]).astype(BF16)
    mnormed[:, 0:1024] = dcatt
    dcq = cq

    @pl.loop(0, 2)
    def _(group):
        d_query, d_keys, d_vals = back_all(
            coarse_of(cq, 0, group),
            coarse_of(cq, 1024, group),
            coarse_of(cq, 2048, group),
            [craised[4 * group + n] for n in range(4)],
            [cinverse[4 * group + n] for n in range(4)],
            coarse_of(catt, 0, group),
            coarse_of(mnormed, 0, group),
        )
        for n in range(4):
            dcq[:, pair_slice(0, 4 * group + n)] = d_query[n]
            dcq[:, pair_slice(1024, 4 * group + n)] = d_keys[n]
            dcq[:, pair_slice(2048, 4 * group + n)] = d_vals[n]

    for step in range(4):
        rows = pl.ds(step * 256, 256)
        cdnorm[:, rows] = nt(dcq[...], cqkv[rows, :])

    d_norm = norm_back(
        c_in[...], cgain, cstat[0][:, 0:1], cstat[1][:, 0:1], cdnorm[:, 0:1024].astype(BF16).astype(F32)
    )
    d_c = (dcot.astype(F32) + d_norm.astype(BF16).astype(F32)).astype(BF16)
    cnormed[...] = d_c

    for step in range(4):
        rows = pl.ds(step * 512, 512)
        cdnorm[:, rows] = nt(cnormed[...], mw[rows, :])

    d_merged = norm_back(
        merged[...], mgain, mstat[0][:, 0:1], mstat[1][:, 0:1], cdnorm[...].astype(BF16).astype(F32)
    ).astype(BF16)
    merged[...] = d_merged
    loads[6].wait()
    total = nn(mrg_t[0], merged[:, 0:512])
    for k in range(1, 4):
        total = total + nn(mrg_t[k], merged[:, 512 * k : 512 * k + 512])
    dmid[...] = total.astype(BF16)

    leave(dmid, dmid_hbm)
    datt[...] = nt(dmid[...], fproj[...]).astype(BF16)
    att_t[...] = att[...].T
    scale_out = 1.0 / math.sqrt(73728)

    for quad in range(4):
        for (_, rows), e_off in zip(PIECES, E_OFF[quad]):
            if rows > 48:
                dqkv[pl.ds(e_off + 48, rows - 48), 0:512] = jnp.zeros((rows - 48, 512), BF16)

    def terms(step, value):
        value = (value * scale_out).astype(BF16)
        low, high = value[:, 0:128], value[:, 128:256]
        for part in range(4):
            rows = slice(128 * part, 128 * part + 128)
            keep[part, step] = jnp.where(core == 0, low[rows], high[rows])
            send[part, step] = jnp.where(core == 0, high[rows], low[rows])

    for step in range(2):
        cols = pl.ds(step * 256, 256)
        terms(6 + step, nn(att_t[...], dmid[:, cols]))

    @pl.loop(0, 4)
    def _(pair):
        d_query, d_keys, d_vals = back_all(
            queries_of(qry, pair),
            keys_of(0, pair),
            keys_of(512, pair),
            [raised_at(index, pair)[...] for index in range(9)],
            [inverse[pair, pl.ds(2 * w[2], 2 * w[3]), :] for w in WINDOWS],
            queries_of(att, pair),
            queries_of(datt, pair),
        )
        for index, (e_off, rows, q_off, q_rows, kind) in enumerate(WINDOWS):
            step = 48 if kind == 3 else 80
            for part in range(q_rows // 48):
                dqkv[pl.ds(e_off + step * part, 48), pair_slice(0, pair)] = d_query[index][
                    48 * part : 48 * part + 48
                ]
            dqkv[pl.ds(e_off, rows), pair_slice(512, pair)] = d_keys[index]
            dqkv[pl.ds(e_off, rows), pair_slice(1024, pair)] = d_vals[index]

    leave(dqkv, dqkv_hbm)

    for step in range(6):
        cols = pl.ds(step * 256, 256)
        terms(step, nn(normed_t[...], dqkv[:, cols]))

    leave(keep, keep_hbm)
    leave(send, send_hbm)
    for copy in leaving:
        copy.wait()


def tokens_kernel(*refs):
    sources, outs, targets = refs[:7], refs[7:11], refs[11:18]
    built, padded, dnorm, sems, row_sems, out_sems = refs[18:]
    gain_in, fqkv, dqkv, dmid, cback, x, expand = targets
    copies = pull(sources[:2], targets[:2], sems)
    rows_in = []
    for part in range(4):
        rows = pl.ds(352 * part, 352)
        rows_in.append(
            pltpu.make_async_copy(sources[2].at[rows], dqkv.at[rows], row_sems.at[part])
        )
        rows_in[-1].start()
    for number in range(3, 7):
        copies.append(pltpu.make_async_copy(sources[number], targets[number], sems.at[number]))
        copies[-1].start()
    copies[0].wait()
    copies[1].wait()
    gain = gain_in[...].astype(F32).reshape(1, 512)
    for part in range(4):
        rows_in[part].wait()
        rows = pl.ds(352 * part, 352)
        dnorm[rows, :] = nt(dqkv[rows, :], fqkv[...])
    for copy in copies[2:]:
        copy.wait()
    pack = one_hot_back(expand[0:1, :], SROWS - TAIL)[:, :304]
    leaving = []
    for quad in (1, 2, 3, 0):
        out = built.at[quad]
        for (start, rows), e_off, q_off in zip(PIECES, E_OFF[quad], Q_OFF[quad]):
            spot = pl.ds(e_off, rows)
            d_norm = norm_back_fresh(x[spot, :], gain, dnorm[spot, :])
            head = d_norm[0:48] + dmid[pl.ds(q_off, 48), :].astype(F32)
            whole = jnp.concatenate([head, d_norm[48:]], axis=0) if rows > 48 else head
            if start == 0:
                out[0:TAIL, :] = whole.astype(BF16)
            else:
                padded[quad, start - TAIL : start - TAIL + rows, :] = whole.astype(BF16)
        padded[quad, 208:304, :] = cback[quad]
        out[TAIL:SROWS, :] = nn(pack, padded[quad]).astype(BF16)
        leaving.append(pltpu.make_async_copy(out, outs[quad], out_sems.at[quad]))
        leaving[-1].start()
    for copy in leaving:
        copy.wait()


def token_grads(*operands):
    return pl.pallas_call(
        tokens_kernel,
        out_shape=(jax.ShapeDtypeStruct((SROWS, 512), BF16),) * 4,
        in_specs=[HBM] * 7,
        out_specs=(HBM,) * 4,
        scratch_shapes=[pltpu.VMEM(value.shape, value.dtype) for value in operands]
        + [
            pltpu.VMEM((4, SROWS, 512), BF16),
            pltpu.VMEM((4, 304, 512), BF16),
            pltpu.VMEM((EXT, 512), F32),
            pltpu.SemaphoreType.DMA((7,)),
            pltpu.SemaphoreType.DMA((4,)),
            pltpu.SemaphoreType.DMA((4,)),
        ],
        cost_estimate=pl.CostEstimate(
            flops=2 * EXT * 1536 * 512, bytes_accessed=24 * 2**20, transcendentals=0
        ),
        compiler_params=pltpu.CompilerParams(vmem_limit_bytes=60 * 2**20),
    )(*operands)


def work(quads, fgain, mgain, cgain, fqkv, fproj, mrg, mrg_t, mw, cqkv, cproj, expand):
    scratch = [
        ((4, SROWS - TAIL, 512), BF16),
        ((8, 384), jnp.int32),
        ((EXT, 512), BF16),
        ((2, CRS, 512), BF16),
        ((512, 1536), BF16),
        ((512, 512), BF16),
        ((4, CRS, QRY), BF16),
        ((4, QRY, CRS), BF16),
        ((2048, 1024), BF16),
        ((1024, 3072), BF16),
        ((1024, 1024), BF16),
        None,
        ((EXT, 512), BF16),
        ((512, EXT), BF16),
        ((EXT, 1024), BF16),
        ((QRY, 512), BF16),
        ((QRY, 512), BF16),
        ((512, QRY), BF16),
        ((4, 4, 96, 144), BF16),
        ((4, 4, 192, 160), BF16),
        ((4, 384, 192), BF16),
        ((4, 2 * QRY, 128), F32),
        ((2, 192, 160), F32),
        ((384, 192), F32),
        ((QRY, 512), BF16),
        ((CRS, 2048), BF16),
        ((2, CRS, 128), F32),
        ((CRS, 2048), BF16),
        ((CRS, 1024), BF16),
        ((2, CRS, 128), F32),
        ((CRS, 1024), BF16),
        ((CRS, 3072), BF16),
        ((CRS, 1024), BF16),
        ((8, 384, 192), BF16),
        ((8, 384, 128), F32),
        ((QRY, 512), BF16),
        ((QRY, 512), BF16),
        ((EXT, 1536), BF16),
        ((CRS, 2048), F32),
        ((4, 96, 512), BF16),
        ((4, 8, 128, 128), BF16),
        ((4, 8, 128, 128), BF16),
        None,
    ]
    scratch = [
        pltpu.SemaphoreType.DMA((31,)) if item is None else pltpu.VMEM(*item) for item in scratch
    ]
    return pl.pallas_call(
        main_kernel,
        out_shape=(
            jax.ShapeDtypeStruct((4, 8, 128, 128), BF16),
            jax.ShapeDtypeStruct((4, 8, 128, 128), BF16),
            jax.ShapeDtypeStruct((EXT, 1536), BF16),
            jax.ShapeDtypeStruct((QRY, 512), BF16),
            jax.ShapeDtypeStruct((4, 96, 512), BF16),
            jax.ShapeDtypeStruct((EXT, 512), BF16),
        ),
        in_specs=[HBM] * 4 + [VMEM] * 3 + [HBM] * 8,
        out_specs=(HBM,) * 6,
        scratch_shapes=scratch,
        compiler_params=pltpu.CompilerParams(vmem_limit_bytes=60 * 2**20),
    )(*quads, fgain, mgain, cgain, fqkv, fproj, mrg, mrg_t, mw, cqkv, cproj, expand)


def shift(value, d_lat, d_lon):
    lats, lons = lax.axis_size("lat"), lax.axis_size("lon")
    pairs = []
    for a in range(lats):
        for b in range(lons):
            source = ((a + d_lat) % lats) * lons + (b + d_lon) % lons
            pairs.append((source, a * lons + b))
    return lax.ppermute(value, ("lat", "lon"), pairs)


def exchange(value, moves):
    lats, lons = lax.axis_size("lat"), lax.axis_size("lon")
    pairs = []
    for a in range(lats):
        for b in range(lons):
            to_a, to_b = moves(a, b)
            pairs.append((a * lons + b, to_a * lons + to_b))
    return lax.ppermute(value, ("lat", "lon"), pairs)


def spread(pieces, moves):
    total = pieces[0].astype(F32)
    for d in (1, 2, 3):
        total = total + exchange(pieces[d], lambda a, b: moves(a, b, d)).astype(F32)
    return total


def pieces_of(value, me):
    return [lax.dynamic_index_in_dim(value, me ^ d, 0, keepdims=False) for d in range(4)]


def local_grads(keep, send, lat):
    got = exchange(send, lambda a, b: (a, b ^ 1))
    pieces = []
    for mine, other in zip(pieces_of(keep, lat // 2), pieces_of(got, lat // 2)):
        pieces.append((mine.astype(F32) + other.astype(F32)).astype(BF16))
    return pieces


def local(
    tokens,
    land_sea,
    land_vec,
    fine_gain,
    fine_qkv,
    fine_proj,
    merge_gain,
    merge_weight,
    coarse_gain,
    coarse_qkv,
    coarse_proj,
    cotangent,
):
    pick, cpick, expand = jnp.asarray(PICK), jnp.asarray(CPICK), jnp.asarray(EXPAND)
    cot = cotangent.transpose(1, 2, 0, 3).reshape(72, 2, 1024)
    sends = prep(tokens.reshape(576, 512), land_sea, land_vec, cot, pick, cpick)
    quads = (sends[0], shift(sends[1], 1, 0), shift(sends[2], 0, 1), shift(sends[3], 1, 1))
    keep, send, dqkv, dmid, cback, x = work(
        quads,
        fine_gain.reshape(1, -1),
        merge_gain.reshape(1, -1),
        coarse_gain.reshape(1, -1),
        fine_qkv,
        fine_proj,
        jnp.asarray(MERGE, BF16),
        jnp.asarray(MERGE.transpose(0, 2, 1), BF16),
        merge_weight,
        coarse_qkv,
        coarse_proj,
        expand,
    )
    lat, lon = lax.axis_index("lat"), lax.axis_index("lon")
    pieces = local_grads(keep, send, lat)
    pieces, dqkv = lax.optimization_barrier((pieces, dqkv))
    back = token_grads(fine_gain, fine_qkv, dqkv, dmid, cback, x, expand)
    terms = spread(pieces, lambda a, b, d: (a ^ (2 * d), b)).astype(BF16)
    terms, _ = lax.optimization_barrier((terms, back))
    moved = (shift(back[1], -1, 0), shift(back[2], 0, -1), shift(back[3], -1, -1))
    terms = pieces_of(terms.reshape(4, 2, 128, 128), lon // 4)
    terms = spread(terms, lambda a, b, d: (a, b ^ (4 * d))).astype(BF16)
    terms, moved = lax.optimization_barrier((terms, moved))
    terms = pieces_of(terms.reshape(4, 64, 128), (lon // 2 % 2) * 2 + lat % 2)
    fine_grads = spread(terms, lambda a, b, d: (a ^ (d & 1), b ^ (d & 2)))
    grad, coarse = finish(pick, cpick, back[0], *moved)
    coarse = coarse.reshape(6, 12, 2, 1024).transpose(2, 0, 1, 3)
    return (coarse, grad.reshape(tokens.shape), fine_grads)


def solution(mesh):
    grid = P(None, "lat", "lon", None)
    placed = (grid, P("lat", "lon")) + (P(),) * 9 + (grid,)
    return jax.shard_map(
        local,
        mesh=mesh,
        in_specs=placed,
        out_specs=(grid, grid, P("lat", "lon")),
        check_vma=False,
    )
```

profile of v0, /device:TPU:0, one launch (start us, length us, event | category | flops | bytes accessed | tf_op | source)
XLA Modules:
  0.0 112.8 jit_solution(1939742043601070990)
XLA Ops:
  0.6 4.1 %shard_map.184 = (bf16[400,512]{1,0:T(8,128)(2,1)}, bf16[400,512]{1,0:T(8,128)(2,1)}, bf16[400,512]{1,0:T(8,128)(2,1)}, bf16[400,512]{1,0:T(8,128)(2,1)}) custom-call(bf16[576,512]{1,0:T(8,128)(2,1)} %bitcast.38, s32[12,24]{1,0:T(8,128)} %refs_1_.3, bf16[512]{0:T(512)(128)(2,1)} %refs_2_.1, bf16[72,2,1024]{2,1,0:T(2,128)(2,1)} %bitcast.39, ...), custom_call_target="tpu_custom_call" | custom-call | tf_op jit(solution)/shard_map/pallas_call | solution.py:194
  4.7 3.9 %collective-permute-start = (bf16[400,512]{1,0:T(8,128)(2,1)}, bf16[400,512]{1,0:T(8,128)(2,1)S(1)}, u32[]{:S(2)}, u32[]{:S(2)}) collective-permute-start(bf16[400,512]{1,0:T(8,128)(2,1)} %get-tuple-element.30), channel_id=1, source_target_pairs={{16,0},{17,1},{18,2},{19,3},{20,4},{21,5},{22,6},{23,7},{24,8},{25... | collective-permute-start | bytes 1228808 | tf_op jit(solution)/shard_map/ppermute | solution.py:817
  8.7 5.5 %collective-permute-start.1 = (bf16[400,512]{1,0:T(8,128)(2,1)}, bf16[400,512]{1,0:T(8,128)(2,1)S(1)}, u32[]{:S(2)}, u32[]{:S(2)}) collective-permute-start(bf16[400,512]{1,0:T(8,128)(2,1)} %get-tuple-element.31), channel_id=1, source_target_pairs={{1,0},{2,1},{3,2},{4,3},{5,4},{6,5},{7,6},{8,7},{9,8},{10,9},{11,1... | collective-permute-start | bytes 1228808 | tf_op jit(solution)/shard_map/ppermute | solution.py:817
  14.4 1.3 %reshape.55.fgain_ref = bf16[1,512]{1,0:T(2,128)(2,1)} reshape(bf16[512]{0:T(512)(128)(2,1)} %refs_0_.2) | data formatting | bytes 2048 | tf_op jit(solution)/shard_map/reshape | solution.py:869
  15.7 1.3 %reshape.56.mgain_ref = bf16[1,2048]{1,0:T(2,128)(2,1)} reshape(bf16[2048]{0:T(1024)(128)(2,1)} %param.23) | data formatting | bytes 8192 | tf_op jit(solution)/shard_map/reshape | solution.py:870
  17.0 1.3 %reshape.57.cgain_ref = bf16[1,1024]{1,0:T(2,128)(2,1)} reshape(bf16[1024]{0:T(1024)(128)(2,1)} %param.25) | data formatting | bytes 4096 | tf_op jit(solution)/shard_map/reshape | solution.py:871
  18.2 0.6 collective-permute-done.q1_ref
  18.9 6.3 %collective-permute-done.1.q2_ref = bf16[400,512]{1,0:T(8,128)(2,1)S(1)} collective-permute-done((bf16[400,512]{1,0:T(8,128)(2,1)}, bf16[400,512]{1,0:T(8,128)(2,1)S(1)}, u32[]{:S(2)}, u32[]{:S(2)}) %collective-permute-start.1) | collective-permute-done | bytes 409632 | tf_op jit(solution)/shard_map/ppermute | solution.py:817
  25.2 1.3 %collective-permute-done.2.q3_ref = bf16[400,512]{1,0:T(8,128)(2,1)S(1)} collective-permute-done((bf16[400,512]{1,0:T(8,128)(2,1)}, bf16[400,512]{1,0:T(8,128)(2,1)S(1)}, u32[]{:S(2)}, u32[]{:S(2)}) %collective-permute-start.2) | collective-permute-done | bytes 409632 | tf_op jit(solution)/shard_map/ppermute | solution.py:817
  26.5 0.8 copy-done.5
  27.3 35.6 %shard_map.185 = (bf16[4,8,128,128]{3,2,1,0:T(8,128)(2,1)}, bf16[4,8,128,128]{3,2,1,0:T(8,128)(2,1)}, bf16[1408,1536]{1,0:T(8,128)(2,1)}, bf16[768,512]{1,0:T(8,...) custom-call(bf16[400,512]{1,0:T(8,128)(2,1)} %get-tuple-element.29.q0_ref, bf16[400,512]{1,0:T(8,128)(2,1)} %copy-done.3, ...), custom_call_target="tpu_custom_call" | custom-call | tf_op jit(solution)/shard_map/pallas_call | solution.py:793
  62.9 1.9 %collective-permute-start.3 = (bf16[4,8,128,128]{3,2,1,0:T(8,128)(2,1)}, bf16[4,8,128,128]{3,2,1,0:T(8,128)(2,1)S(1)}, u32[]{:S(2)}, u32[]{:S(2)}) collective-permute-start(bf16[4,8,128,128]{3,2,1,0:T(8,128)(2,1)} %get-tuple-element.34), channel_id=1, source_target_pairs={{0,1},{1,0},{2,3},{3,2},{4,5},{5,4},{6,7},{7,6},{8,9},{9,8},{10,11... | collective-permute-start | bytes 3145736 | tf_op jit(solution)/shard_map/ppermute | solution.py:827
  64.9 2.5 %collective-permute-done.3 = bf16[4,8,128,128]{3,2,1,0:T(8,128)(2,1)S(1)} collective-permute-done((bf16[4,8,128,128]{3,2,1,0:T(8,128)(2,1)}, bf16[4,8,128,128]{3,2,1,0:T(8,128)(2,1)S(1)}, u32[]{:S(2)}, u32[]{:S(2)}) %collective-permute-start.3) | collective-permute-done | bytes 1048608 | tf_op jit(solution)/shard_map/ppermute | solution.py:827
  67.3 1.5 %fusion.3 = (bf16[8,128,128]{2,1,0:T(8,128)(2,1)S(1)}, bf16[8,128,128]{2,1,0:T(8,128)(2,1)S(1)}, bf16[8,128,128]{2,1,0:T(8,128)(2,1)S(1)}, bf16[8,128,128]{2,1,0:T(8,128)(2,1)S(1)}) fusion(bf16[4,8,128,128]{3,2,1,0:T(8,128)(2,1)S(1)} %collective-permute-done.3, s32[]{:T(128)S(6)} %select_n.69, bf16[4,8,128,128]{3,2,1,0:T(8,128)(2,1)} %get-tuple-element.33, ...), kind=kLoop, calls=%fused_computation.8 | loop fusion | flops 2097152 | bytes 3145744 | tf_op jit(solution)/shard_map/convert_element_type | solution.py:845
  68.9 3.4 %collective-permute-start.6 = (bf16[8,128,128]{2,1,0:T(8,128)(2,1)S(1)}, bf16[8,128,128]{2,1,0:T(8,128)(2,1)S(1)}, u32[]{:S(2)}, u32[]{:S(2)}) collective-permute-start(bf16[8,128,128]{2,1,0:T(8,128)(2,1)S(1)} %get-tuple-element.44), channel_id=1, source_target_pairs={{0,96},{1,97},{2,98},{3,99},{4,100},{5,101},{6,102},{7,103},{8,104... | collective-permute-start | bytes 786440 | tf_op jit(solution)/shard_map/ppermute | solution.py:827
  72.3 0.3 collective-permute-start.5
  72.5 0.7 collective-permute-start.4
  73.2 7.8 %shard_map.186 = (bf16[400,512]{1,0:T(8,128)(2,1)}, bf16[400,512]{1,0:T(8,128)(2,1)}, bf16[400,512]{1,0:T(8,128)(2,1)}, bf16[400,512]{1,0:T(8,128)(2,1)}) custom-call(bf16[512]{0:T(512)(128)(2,1)} %refs_0_.2, bf16[512,1536]{1,0:T(8,128)(2,1)} %refs_1_.4, bf16[1408,1536]{1,0:T(8,128)(2,1)} %get-tuple-element.36.refs_2_, ...), custom_call_target="tpu_custom_call" | custom-call | flops 2214592512 | bytes 25165824 | tf_op jit(solution)/shard_map/pallas_call | solution.py:723
  81.0 0.8 collective-permute-start.10
  81.8 2.9 %collective-permute-done.6 = bf16[8,128,128]{2,1,0:T(8,128)(2,1)S(1)} collective-permute-done((bf16[8,128,128]{2,1,0:T(8,128)(2,1)S(1)}, bf16[8,128,128]{2,1,0:T(8,128)(2,1)S(1)}, u32[]{:S(2)}, u32[]{:S(2)}) %collective-permute-start.6) | collective-permute-done | bytes 262176 | tf_op jit(solution)/shard_map/ppermute | solution.py:827
  84.7 0.7 collective-permute-start.12
  85.6 4.1 %collective-permute-start.9 = (bf16[2,128,128]{2,1,0:T(8,128)(2,1)S(1)}, bf16[2,128,128]{2,1,0:T(8,128)(2,1)S(1)}, u32[]{:S(2)}, u32[]{:S(2)}) collective-permute-start(bf16[2,128,128]{2,1,0:T(8,128)(2,1)S(1)} %get-tuple-element.60), channel_id=1, source_target_pairs={{0,12},{1,13},{2,14},{3,15},{4,8},{5,9},{6,10},{7,11},{8,4},{9,5},... | collective-permute-start | bytes 196616 | tf_op jit(solution)/shard_map/ppermute | solution.py:827
  89.7 3.2 %collective-permute-done.9 = bf16[2,128,128]{2,1,0:T(8,128)(2,1)S(1)} collective-permute-done((bf16[2,128,128]{2,1,0:T(8,128)(2,1)S(1)}, bf16[2,128,128]{2,1,0:T(8,128)(2,1)S(1)}, u32[]{:S(2)}, u32[]{:S(2)}) %collective-permute-start.9) | collective-permute-done | bytes 65568 | tf_op jit(solution)/shard_map/ppermute | solution.py:827
  92.9 2.9 %collective-permute-done.8 = bf16[2,128,128]{2,1,0:T(8,128)(2,1)S(1)} collective-permute-done((bf16[2,128,128]{2,1,0:T(8,128)(2,1)S(1)}, bf16[2,128,128]{2,1,0:T(8,128)(2,1)S(1)}, u32[]{:S(2)}, u32[]{:S(2)}) %collective-permute-start.8) | collective-permute-done | bytes 65568 | tf_op jit(solution)/shard_map/ppermute | solution.py:827
  95.8 6.9 %collective-permute-done.7 = bf16[2,128,128]{2,1,0:T(8,128)(2,1)S(1)} collective-permute-done((bf16[2,128,128]{2,1,0:T(8,128)(2,1)S(1)}, bf16[2,128,128]{2,1,0:T(8,128)(2,1)S(1)}, u32[]{:S(2)}, u32[]{:S(2)}) %collective-permute-start.7) | collective-permute-done | bytes 65568 | tf_op jit(solution)/shard_map/ppermute | solution.py:827
  102.8 0.5 collective-permute-done.11.refs_4_
  103.3 1.1 collective-permute-done.12.refs_5_
  104.4 0.4 collective-permute-start.15
  104.9 2.5 %collective-permute-start.14 = (bf16[64,128]{1,0:T(8,128)(2,1)S(1)}, bf16[64,128]{1,0:T(8,128)(2,1)S(1)}, u32[]{:S(2)}, u32[]{:S(2)}) collective-permute-start(bf16[64,128]{1,0:T(8,128)(2,1)S(1)} %get-tuple-element.64), channel_id=1, source_target_pairs={{0,2},{1,3},{2,0},{3,1},{4,6},{5,7},{6,4},{7,5},{8,10},{9,11},{10,... | collective-permute-start | bytes 49160 | tf_op jit(solution)/shard_map/ppermute | solution.py:827
  107.4 1.2 %collective-permute-start.13 = (bf16[64,128]{1,0:T(8,128)(2,1)S(1)}, bf16[64,128]{1,0:T(8,128)(2,1)S(1)}, u32[]{:S(2)}, u32[]{:S(2)}) collective-permute-start(bf16[64,128]{1,0:T(8,128)(2,1)S(1)} %get-tuple-element.62), channel_id=1, source_target_pairs={{0,16},{1,17},{2,18},{3,19},{4,20},{5,21},{6,22},{7,23},{8,24},{9,... | collective-permute-start | bytes 49160 | tf_op jit(solution)/shard_map/ppermute | solution.py:827
  108.6 3.6 %shard_map.187 = (bf16[576,512]{1,0:T(8,128)(2,1)}, bf16[72,2,1024]{2,1,0:T(2,128)(2,1)}) custom-call(s32[8,384]{1,0:T(8,128)} %constant.107.clone.refs_4_.refs_0_, s32[16,128]{1,0:T(8,128)} %constant.108.clone.refs_5_.refs_1_, bf16[400,512]{1,0:T(8,128)(2,1)} %get-tuple-element.40.refs_2_, bf16[400,512]{1,0:T(8,128)(2,1)} %copy-done, ...), custom_call_target="tpu_custom_call" | custom-call | tf_op jit(solution)/shard_map/pallas_call | solution.py:241
  112.2 0.6 fusion.8
  (25 shorter events, 0.5 us)
Async XLA Ops:
  4.7 14.2 %collective-permute-start = (bf16[400,512]{1,0:T(8,128)(2,1)}, bf16[400,512]{1,0:T(8,128)(2,1)S(1)}, u32[]{:S(2)}, u32[]{:S(2)}) collective-permute-start(bf16[400,512]{1,0:T(8,128)(2,1)} %get-tuple-element.30), channel_id=1, source_target_pairs={{16,0},{17,1},{18,2},{19,3},{20,4},{21,5},{22,6},{23,7},{24,8},{25... | collective-permute-start | bytes 1228808 | tf_op jit(solution)/shard_map/ppermute | solution.py:817
  8.7 16.5 %collective-permute-start.1 = (bf16[400,512]{1,0:T(8,128)(2,1)}, bf16[400,512]{1,0:T(8,128)(2,1)S(1)}, u32[]{:S(2)}, u32[]{:S(2)}) collective-permute-start(bf16[400,512]{1,0:T(8,128)(2,1)} %get-tuple-element.31), channel_id=1, source_target_pairs={{1,0},{2,1},{3,2},{4,3},{5,4},{6,5},{7,6},{8,7},{9,8},{10,9},{11,1... | collective-permute-start | bytes 1228808 | tf_op jit(solution)/shard_map/ppermute | solution.py:817
  14.2 12.3 %collective-permute-start.2 = (bf16[400,512]{1,0:T(8,128)(2,1)}, bf16[400,512]{1,0:T(8,128)(2,1)S(1)}, u32[]{:S(2)}, u32[]{:S(2)}) collective-permute-start(bf16[400,512]{1,0:T(8,128)(2,1)} %get-tuple-element.32), channel_id=1, source_target_pairs={{17,0},{18,1},{19,2},{20,3},{21,4},{22,5},{23,6},{24,7},{25,8},{26... | collective-permute-start | bytes 1228808 | tf_op jit(solution)/shard_map/ppermute | solution.py:817
  18.9 7.6 %copy-start.3 = (bf16[400,512]{1,0:T(8,128)(2,1)}, bf16[400,512]{1,0:T(8,128)(2,1)S(1)}, u32[]{:S(2)}) copy-start(bf16[400,512]{1,0:T(8,128)(2,1)S(1)} %collective-permute-done.q1_ref) | copy-start | bytes 1228804
  25.2 1.4 %copy-start.4 = (bf16[400,512]{1,0:T(8,128)(2,1)}, bf16[400,512]{1,0:T(8,128)(2,1)S(1)}, u32[]{:S(2)}) copy-start(bf16[400,512]{1,0:T(8,128)(2,1)S(1)} %collective-permute-done.1.q2_ref) | copy-start | bytes 1228804
  26.5 0.8 copy-start.5
  62.9 4.4 %collective-permute-start.3 = (bf16[4,8,128,128]{3,2,1,0:T(8,128)(2,1)}, bf16[4,8,128,128]{3,2,1,0:T(8,128)(2,1)S(1)}, u32[]{:S(2)}, u32[]{:S(2)}) collective-permute-start(bf16[4,8,128,128]{3,2,1,0:T(8,128)(2,1)} %get-tuple-element.34), channel_id=1, source_target_pairs={{0,1},{1,0},{2,3},{3,2},{4,5},{5,4},{6,7},{7,6},{8,9},{9,8},{10,11... | collective-permute-start | bytes 3145736 | tf_op jit(solution)/shard_map/ppermute | solution.py:827
  68.9 15.8 %collective-permute-start.6 = (bf16[8,128,128]{2,1,0:T(8,128)(2,1)S(1)}, bf16[8,128,128]{2,1,0:T(8,128)(2,1)S(1)}, u32[]{:S(2)}, u32[]{:S(2)}) collective-permute-start(bf16[8,128,128]{2,1,0:T(8,128)(2,1)S(1)} %get-tuple-element.44), channel_id=1, source_target_pairs={{0,96},{1,97},{2,98},{3,99},{4,100},{5,101},{6,102},{7,103},{8,104... | collective-permute-start | bytes 786440 | tf_op jit(solution)/shard_map/ppermute | solution.py:827
  72.3 13.2 %collective-permute-start.5 = (bf16[8,128,128]{2,1,0:T(8,128)(2,1)S(1)}, bf16[8,128,128]{2,1,0:T(8,128)(2,1)S(1)}, u32[]{:S(2)}, u32[]{:S(2)}) collective-permute-start(bf16[8,128,128]{2,1,0:T(8,128)(2,1)S(1)} %get-tuple-element.43), channel_id=1, source_target_pairs={{0,64},{1,65},{2,66},{3,67},{4,68},{5,69},{6,70},{7,71},{8,72},{9,... | collective-permute-start | bytes 786440 | tf_op jit(solution)/shard_map/ppermute | solution.py:827
  72.5 12.9 %collective-permute-start.4 = (bf16[8,128,128]{2,1,0:T(8,128)(2,1)S(1)}, bf16[8,128,128]{2,1,0:T(8,128)(2,1)S(1)}, u32[]{:S(2)}, u32[]{:S(2)}) collective-permute-start(bf16[8,128,128]{2,1,0:T(8,128)(2,1)S(1)} %get-tuple-element.42), channel_id=1, source_target_pairs={{0,32},{1,33},{2,34},{3,35},{4,36},{5,37},{6,38},{7,39},{8,40},{9,... | collective-permute-start | bytes 786440 | tf_op jit(solution)/shard_map/ppermute | solution.py:827
  81.0 21.8 %collective-permute-start.10 = (bf16[400,512]{1,0:T(8,128)(2,1)}, bf16[400,512]{1,0:T(8,128)(2,1)S(1)}, u32[]{:S(2)}, u32[]{:S(2)}) collective-permute-start(bf16[400,512]{1,0:T(8,128)(2,1)} %get-tuple-element.45), channel_id=1, source_target_pairs={{112,0},{113,1},{114,2},{115,3},{116,4},{117,5},{118,6},{119,7},{1... | collective-permute-start | bytes 1228808 | tf_op jit(solution)/shard_map/ppermute | solution.py:817
  81.8 21.5 %collective-permute-start.11 = (bf16[400,512]{1,0:T(8,128)(2,1)}, bf16[400,512]{1,0:T(8,128)(2,1)S(1)}, u32[]{:S(2)}, u32[]{:S(2)}) collective-permute-start(bf16[400,512]{1,0:T(8,128)(2,1)} %get-tuple-element.46), channel_id=1, source_target_pairs={{15,0},{0,1},{1,2},{2,3},{3,4},{4,5},{5,6},{6,7},{7,8},{8,9},{9,10... | collective-permute-start | bytes 1228808 | tf_op jit(solution)/shard_map/ppermute | solution.py:817
  84.7 19.7 %collective-permute-start.12 = (bf16[400,512]{1,0:T(8,128)(2,1)}, bf16[400,512]{1,0:T(8,128)(2,1)S(1)}, u32[]{:S(2)}, u32[]{:S(2)}) collective-permute-start(bf16[400,512]{1,0:T(8,128)(2,1)} %get-tuple-element.47), channel_id=1, source_target_pairs={{127,0},{112,1},{113,2},{114,3},{115,4},{116,5},{117,6},{118,7},{1... | collective-permute-start | bytes 1228808 | tf_op jit(solution)/shard_map/ppermute | solution.py:817
  85.6 7.3 %collective-permute-start.9 = (bf16[2,128,128]{2,1,0:T(8,128)(2,1)S(1)}, bf16[2,128,128]{2,1,0:T(8,128)(2,1)S(1)}, u32[]{:S(2)}, u32[]{:S(2)}) collective-permute-start(bf16[2,128,128]{2,1,0:T(8,128)(2,1)S(1)} %get-tuple-element.60), channel_id=1, source_target_pairs={{0,12},{1,13},{2,14},{3,15},{4,8},{5,9},{6,10},{7,11},{8,4},{9,5},... | collective-permute-start | bytes 196616 | tf_op jit(solution)/shard_map/ppermute | solution.py:827
  89.7 6.1 %collective-permute-start.8 = (bf16[2,128,128]{2,1,0:T(8,128)(2,1)S(1)}, bf16[2,128,128]{2,1,0:T(8,128)(2,1)S(1)}, u32[]{:S(2)}, u32[]{:S(2)}) collective-permute-start(bf16[2,128,128]{2,1,0:T(8,128)(2,1)S(1)} %get-tuple-element.61), channel_id=1, source_target_pairs={{0,8},{1,9},{2,10},{3,11},{4,12},{5,13},{6,14},{7,15},{8,0},{9,1},... | collective-permute-start | bytes 196616 | tf_op jit(solution)/shard_map/ppermute | solution.py:827
  92.9 9.8 %collective-permute-start.7 = (bf16[2,128,128]{2,1,0:T(8,128)(2,1)S(1)}, bf16[2,128,128]{2,1,0:T(8,128)(2,1)S(1)}, u32[]{:S(2)}, u32[]{:S(2)}) collective-permute-start(bf16[2,128,128]{2,1,0:T(8,128)(2,1)S(1)} %get-tuple-element.59), channel_id=1, source_target_pairs={{0,4},{1,5},{2,6},{3,7},{4,0},{5,1},{6,2},{7,3},{8,12},{9,13},{10,... | collective-permute-start | bytes 196616 | tf_op jit(solution)/shard_map/ppermute | solution.py:827
  102.8 5.8 %copy-start = (bf16[400,512]{1,0:T(8,128)(2,1)}, bf16[400,512]{1,0:T(8,128)(2,1)S(1)}, u32[]{:S(2)}) copy-start(bf16[400,512]{1,0:T(8,128)(2,1)S(1)} %collective-permute-done.10.refs_3_) | copy-start | bytes 1228804
  103.3 5.3 %copy-start.1 = (bf16[400,512]{1,0:T(8,128)(2,1)}, bf16[400,512]{1,0:T(8,128)(2,1)S(1)}, u32[]{:S(2)}) copy-start(bf16[400,512]{1,0:T(8,128)(2,1)S(1)} %collective-permute-done.11.refs_4_) | copy-start | bytes 1228804
  104.4 4.2 %copy-start.2 = (bf16[400,512]{1,0:T(8,128)(2,1)}, bf16[400,512]{1,0:T(8,128)(2,1)S(1)}, u32[]{:S(2)}) copy-start(bf16[400,512]{1,0:T(8,128)(2,1)S(1)} %collective-permute-done.12.refs_5_) | copy-start | bytes 1228804
  104.4 7.8 %collective-permute-start.15 = (bf16[64,128]{1,0:T(8,128)(2,1)S(1)}, bf16[64,128]{1,0:T(8,128)(2,1)S(1)}, u32[]{:S(2)}, u32[]{:S(2)}) collective-permute-start(bf16[64,128]{1,0:T(8,128)(2,1)S(1)} %get-tuple-element.63), channel_id=1, source_target_pairs={{0,18},{1,19},{2,16},{3,17},{4,22},{5,23},{6,20},{7,21},{8,26},{9,... | collective-permute-start | bytes 49160 | tf_op jit(solution)/shard_map/ppermute | solution.py:827
  104.9 7.3 %collective-permute-start.14 = (bf16[64,128]{1,0:T(8,128)(2,1)S(1)}, bf16[64,128]{1,0:T(8,128)(2,1)S(1)}, u32[]{:S(2)}, u32[]{:S(2)}) collective-permute-start(bf16[64,128]{1,0:T(8,128)(2,1)S(1)} %get-tuple-element.64), channel_id=1, source_target_pairs={{0,2},{1,3},{2,0},{3,1},{4,6},{5,7},{6,4},{7,5},{8,10},{9,11},{10,... | collective-permute-start | bytes 49160 | tf_op jit(solution)/shard_map/ppermute | solution.py:827
  107.4 4.8 %collective-permute-start.13 = (bf16[64,128]{1,0:T(8,128)(2,1)S(1)}, bf16[64,128]{1,0:T(8,128)(2,1)S(1)}, u32[]{:S(2)}, u32[]{:S(2)}) collective-permute-start(bf16[64,128]{1,0:T(8,128)(2,1)S(1)} %get-tuple-element.62), channel_id=1, source_target_pairs={{0,16},{1,17},{2,18},{3,19},{4,20},{5,21},{6,22},{7,23},{8,24},{9,... | collective-permute-start | bytes 49160 | tf_op jit(solution)/shard_map/ppermute | solution.py:827
where the time goes:
time: 114 us; the launch traced here: 113 us
  Pallas kernels  51.1 us (45%)
  waiting for transfers between devices  28.3 us (25%)
  starting transfers between devices  25.7 us (23%)
  local copies, waits for them, and re-layouts  4.62 us (4%)
  other arithmetic  2.36 us (2%)
    pallas_call x1, Pallas kernels, work(): pl.pallas_call(main_kernel, out_shape=(jax.ShapeDtypeStruct((4, 8, 128, 1...  35.6 us
    ppermute x10, waiting for transfers between devices, exchange(): return lax.ppermute(value, ('lat', 'lon'), pairs)  18.4 us
    ppermute x10, starting transfers between devices, exchange(): return lax.ppermute(value, ('lat', 'lon'), pairs)  14.5 us
    ppermute x6, starting transfers between devices, shift(): return lax.ppermute(value, ('lat', 'lon'), pairs)  11.2 us
    ppermute x6, waiting for transfers between devices, shift(): return lax.ppermute(value, ('lat', 'lon'), pairs)  9.88 us
    pallas_call x1, Pallas kernels, token_grads(): pl.pallas_call(tokens_kernel, out_shape=(jax.ShapeDtypeStruct((SROWS, 512...  7.81 us
    pallas_call x1, Pallas kernels, prep(): pl.pallas_call(prep_kernel, out_shape=(jax.ShapeDtypeStruct((SROWS, 512),...  4.09 us
    pallas_call x1, Pallas kernels, finish(): pl.pallas_call(finish_kernel, out_shape=(jax.ShapeDtypeStruct((576, 512),...  3.57 us
  transfers between devices with their start and end apart: 16, of which 10 were waited for; matrix products, arithmetic and copies ran while one was open for 4% of the time, Pallas kernels for 10%

commit v1 on v0

--- a/solution.py
+++ b/solution.py
@@ -319,6 +319,8 @@
 
 
 def pair_slice(start, pair):
+    if isinstance(pair, int):
+        return pl.ds(start + pair * 128, 128)
     return pl.ds(pl.multiple_of(start + pair * 128, 128), 128)
 
 
@@ -477,9 +479,8 @@
             normed[...], fqkv[:, pl.ds(512 + step * 256, 256)]
         ).astype(BF16)
 
-    @pl.loop(0, 2)
-    def _(step):
-        cols = pl.ds(pl.multiple_of(step * 256, 256), 256)
+    for step in range(2):
+        cols = pl.ds(step * 256, 256)
         left = cells(lambda off: normed[pl.ds(off, 48), :])
         qry[:, cols] = (nn(left, fqkv[:, cols]).astype(BF16) * 0.125).astype(BF16)
 
@@ -517,9 +518,8 @@
 
     loads[1].wait()
 
-    @pl.loop(0, 2)
-    def _(step):
-        cols = pl.ds(pl.multiple_of(step * 256, 256), 256)
+    for step in range(2):
+        cols = pl.ds(step * 256, 256)
         left = cells(lambda off: x[pl.ds(off, 48), cols])
         mid[:, cols] = (left.astype(F32) + nn(att[...], fproj[:, cols])).astype(BF16)
 
@@ -552,8 +552,7 @@
     def coarse_of(ref, start, group):
         return [ref[:, pair_slice(start, 4 * group + n)] for n in range(4)]
 
-    @pl.loop(0, 2)
-    def _(group):
+    for group in range(2):
         raised, inv, mixed = attend_all(
             coarse_of(cq, 0, group),
             coarse_of(cq, 1024, group),
@@ -580,8 +579,7 @@
     mnormed[:, 0:1024] = dcatt
     dcq = cq
 
-    @pl.loop(0, 2)
-    def _(group):
+    for group in range(2):
         d_query, d_keys, d_vals = back_all(
             coarse_of(cq, 0, group),
             coarse_of(cq, 1024, group),

time: 114 us -> 112 us (0.982)
  Pallas kernels: 51.1 us -> 49 us
    pallas_call x1, Pallas kernels: 35.6 us -> 33.6 us  [work(): pl.pallas_call(main_kernel, out_shape=(jax.ShapeDtypeStruct((4, 8, 128, 1...]
where the time goes in v1:
time: 112 us; the launch traced here: 111 us
  Pallas kernels  49 us (44%)
  waiting for transfers between devices  28.3 us (25%)
  starting transfers between devices  25.7 us (23%)
  local copies, waits for them, and re-layouts  4.62 us (4%)
  other arithmetic  2.36 us (2%)
    pallas_call x1, Pallas kernels, work(): pl.pallas_call(main_kernel, out_shape=(jax.ShapeDtypeStruct((4, 8, 128, 1...  33.6 us
    ppermute x10, waiting for transfers between devices, exchange(): return lax.ppermute(value, ('lat', 'lon'), pairs)  18.5 us
    ppermute x10, starting transfers between devices, exchange(): return lax.ppermute(value, ('lat', 'lon'), pairs)  14.5 us
    ppermute x6, starting transfers between devices, shift(): return lax.ppermute(value, ('lat', 'lon'), pairs)  11.2 us
    ppermute x6, waiting for transfers between devices, shift(): return lax.ppermute(value, ('lat', 'lon'), pairs)  9.87 us
    pallas_call x1, Pallas kernels, token_grads(): pl.pallas_call(tokens_kernel, out_shape=(jax.ShapeDtypeStruct((SROWS, 512...  7.79 us
    pallas_call x1, Pallas kernels, prep(): pl.pallas_call(prep_kernel, out_shape=(jax.ShapeDtypeStruct((SROWS, 512),...  4.09 us
    pallas_call x1, Pallas kernels, finish(): pl.pallas_call(finish_kernel, out_shape=(jax.ShapeDtypeStruct((576, 512),...  3.57 us
  transfers between devices with their start and end apart: 16, of which 10 were waited for; matrix products, arithmetic and copies ran while one was open for 4% of the time, Pallas kernels for 10%

profile of v1, /device:TPU:0, one launch (start us, length us, event | category | flops | bytes accessed | tf_op | source)
XLA Modules:
  0.0 110.8 jit_solution(11913556261884298068)
XLA Ops:
  0.6 4.1 %shard_map.184 = (bf16[400,512]{1,0:T(8,128)(2,1)}, bf16[400,512]{1,0:T(8,128)(2,1)}, bf16[400,512]{1,0:T(8,128)(2,1)}, bf16[400,512]{1,0:T(8,128)(2,1)}) custom-call(bf16[576,512]{1,0:T(8,128)(2,1)} %bitcast.38, s32[12,24]{1,0:T(8,128)} %refs_1_.3, bf16[512]{0:T(512)(128)(2,1)} %refs_2_.1, bf16[72,2,1024]{2,1,0:T(2,128)(2,1)} %bitcast.39, ...), custom_call_target="tpu_custom_call" | custom-call | tf_op jit(solution)/shard_map/pallas_call | solution.py:194
  4.7 3.9 %collective-permute-start = (bf16[400,512]{1,0:T(8,128)(2,1)}, bf16[400,512]{1,0:T(8,128)(2,1)S(1)}, u32[]{:S(2)}, u32[]{:S(2)}) collective-permute-start(bf16[400,512]{1,0:T(8,128)(2,1)} %get-tuple-element.30), channel_id=1, source_target_pairs={{16,0},{17,1},{18,2},{19,3},{20,4},{21,5},{22,6},{23,7},{24,8},{25... | collective-permute-start | bytes 1228808 | tf_op jit(solution)/shard_map/ppermute | solution.py:815
  8.7 5.5 %collective-permute-start.1 = (bf16[400,512]{1,0:T(8,128)(2,1)}, bf16[400,512]{1,0:T(8,128)(2,1)S(1)}, u32[]{:S(2)}, u32[]{:S(2)}) collective-permute-start(bf16[400,512]{1,0:T(8,128)(2,1)} %get-tuple-element.31), channel_id=1, source_target_pairs={{1,0},{2,1},{3,2},{4,3},{5,4},{6,5},{7,6},{8,7},{9,8},{10,9},{11,1... | collective-permute-start | bytes 1228808 | tf_op jit(solution)/shard_map/ppermute | solution.py:815
  14.4 1.3 %reshape.55.fgain_ref = bf16[1,512]{1,0:T(2,128)(2,1)} reshape(bf16[512]{0:T(512)(128)(2,1)} %refs_0_.2) | data formatting | bytes 2048 | tf_op jit(solution)/shard_map/reshape | solution.py:867
  15.7 1.3 %reshape.56.mgain_ref = bf16[1,2048]{1,0:T(2,128)(2,1)} reshape(bf16[2048]{0:T(1024)(128)(2,1)} %param.23) | data formatting | bytes 8192 | tf_op jit(solution)/shard_map/reshape | solution.py:868
  17.0 1.3 %reshape.57.cgain_ref = bf16[1,1024]{1,0:T(2,128)(2,1)} reshape(bf16[1024]{0:T(1024)(128)(2,1)} %param.25) | data formatting | bytes 4096 | tf_op jit(solution)/shard_map/reshape | solution.py:869
  18.2 0.6 collective-permute-done.q1_ref
  18.9 6.3 %collective-permute-done.1.q2_ref = bf16[400,512]{1,0:T(8,128)(2,1)S(1)} collective-permute-done((bf16[400,512]{1,0:T(8,128)(2,1)}, bf16[400,512]{1,0:T(8,128)(2,1)S(1)}, u32[]{:S(2)}, u32[]{:S(2)}) %collective-permute-start.1) | collective-permute-done | bytes 409632 | tf_op jit(solution)/shard_map/ppermute | solution.py:815
  25.2 1.3 %collective-permute-done.2.q3_ref = bf16[400,512]{1,0:T(8,128)(2,1)S(1)} collective-permute-done((bf16[400,512]{1,0:T(8,128)(2,1)}, bf16[400,512]{1,0:T(8,128)(2,1)S(1)}, u32[]{:S(2)}, u32[]{:S(2)}) %collective-permute-start.2) | collective-permute-done | bytes 409632 | tf_op jit(solution)/shard_map/ppermute | solution.py:815
  26.5 0.8 copy-done.5
  27.3 33.6 %shard_map.185 = (bf16[4,8,128,128]{3,2,1,0:T(8,128)(2,1)}, bf16[4,8,128,128]{3,2,1,0:T(8,128)(2,1)}, bf16[1408,1536]{1,0:T(8,128)(2,1)}, bf16[768,512]{1,0:T(8,...) custom-call(bf16[400,512]{1,0:T(8,128)(2,1)} %get-tuple-element.29.q0_ref, bf16[400,512]{1,0:T(8,128)(2,1)} %copy-done.3, ...), custom_call_target="tpu_custom_call" | custom-call | tf_op jit(solution)/shard_map/pallas_call | solution.py:791
  60.9 1.9 %collective-permute-start.3 = (bf16[4,8,128,128]{3,2,1,0:T(8,128)(2,1)}, bf16[4,8,128,128]{3,2,1,0:T(8,128)(2,1)S(1)}, u32[]{:S(2)}, u32[]{:S(2)}) collective-permute-start(bf16[4,8,128,128]{3,2,1,0:T(8,128)(2,1)} %get-tuple-element.34), channel_id=1, source_target_pairs={{0,1},{1,0},{2,3},{3,2},{4,5},{5,4},{6,7},{7,6},{8,9},{9,8},{10,11... | collective-permute-start | bytes 3145736 | tf_op jit(solution)/shard_map/ppermute | solution.py:825
  62.8 2.5 %collective-permute-done.3 = bf16[4,8,128,128]{3,2,1,0:T(8,128)(2,1)S(1)} collective-permute-done((bf16[4,8,128,128]{3,2,1,0:T(8,128)(2,1)}, bf16[4,8,128,128]{3,2,1,0:T(8,128)(2,1)S(1)}, u32[]{:S(2)}, u32[]{:S(2)}) %collective-permute-start.3) | collective-permute-done | bytes 1048608 | tf_op jit(solution)/shard_map/ppermute | solution.py:825
  65.3 1.5 %fusion.3 = (bf16[8,128,128]{2,1,0:T(8,128)(2,1)S(1)}, bf16[8,128,128]{2,1,0:T(8,128)(2,1)S(1)}, bf16[8,128,128]{2,1,0:T(8,128)(2,1)S(1)}, bf16[8,128,128]{2,1,0:T(8,128)(2,1)S(1)}) fusion(bf16[4,8,128,128]{3,2,1,0:T(8,128)(2,1)S(1)} %collective-permute-done.3, s32[]{:T(128)S(6)} %select_n.69, bf16[4,8,128,128]{3,2,1,0:T(8,128)(2,1)} %get-tuple-element.33, ...), kind=kLoop, calls=%fused_computation.8 | loop fusion | flops 2097152 | bytes 3145744 | tf_op jit(solution)/shard_map/convert_element_type | solution.py:843
  66.8 3.4 %collective-permute-start.6 = (bf16[8,128,128]{2,1,0:T(8,128)(2,1)S(1)}, bf16[8,128,128]{2,1,0:T(8,128)(2,1)S(1)}, u32[]{:S(2)}, u32[]{:S(2)}) collective-permute-start(bf16[8,128,128]{2,1,0:T(8,128)(2,1)S(1)} %get-tuple-element.44), channel_id=1, source_target_pairs={{0,96},{1,97},{2,98},{3,99},{4,100},{5,101},{6,102},{7,103},{8,104... | collective-permute-start | bytes 786440 | tf_op jit(solution)/shard_map/ppermute | solution.py:825
  70.2 0.3 collective-permute-start.5
  70.5 0.7 collective-permute-start.4
  71.2 7.8 %shard_map.186 = (bf16[400,512]{1,0:T(8,128)(2,1)}, bf16[400,512]{1,0:T(8,128)(2,1)}, bf16[400,512]{1,0:T(8,128)(2,1)}, bf16[400,512]{1,0:T(8,128)(2,1)}) custom-call(bf16[512]{0:T(512)(128)(2,1)} %refs_0_.2, bf16[512,1536]{1,0:T(8,128)(2,1)} %refs_1_.4, bf16[1408,1536]{1,0:T(8,128)(2,1)} %get-tuple-element.36.refs_2_, ...), custom_call_target="tpu_custom_call" | custom-call | flops 2214592512 | bytes 25165824 | tf_op jit(solution)/shard_map/pallas_call | solution.py:721
  79.0 0.8 collective-permute-start.10
  79.8 2.9 %collective-permute-done.6 = bf16[8,128,128]{2,1,0:T(8,128)(2,1)S(1)} collective-permute-done((bf16[8,128,128]{2,1,0:T(8,128)(2,1)S(1)}, bf16[8,128,128]{2,1,0:T(8,128)(2,1)S(1)}, u32[]{:S(2)}, u32[]{:S(2)}) %collective-permute-start.6) | collective-permute-done | bytes 262176 | tf_op jit(solution)/shard_map/ppermute | solution.py:825
  82.6 0.7 collective-permute-start.12
  83.6 4.1 %collective-permute-start.9 = (bf16[2,128,128]{2,1,0:T(8,128)(2,1)S(1)}, bf16[2,128,128]{2,1,0:T(8,128)(2,1)S(1)}, u32[]{:S(2)}, u32[]{:S(2)}) collective-permute-start(bf16[2,128,128]{2,1,0:T(8,128)(2,1)S(1)} %get-tuple-element.60), channel_id=1, source_target_pairs={{0,12},{1,13},{2,14},{3,15},{4,8},{5,9},{6,10},{7,11},{8,4},{9,5},... | collective-permute-start | bytes 196616 | tf_op jit(solution)/shard_map/ppermute | solution.py:825
  87.7 3.2 %collective-permute-done.9 = bf16[2,128,128]{2,1,0:T(8,128)(2,1)S(1)} collective-permute-done((bf16[2,128,128]{2,1,0:T(8,128)(2,1)S(1)}, bf16[2,128,128]{2,1,0:T(8,128)(2,1)S(1)}, u32[]{:S(2)}, u32[]{:S(2)}) %collective-permute-start.9) | collective-permute-done | bytes 65568 | tf_op jit(solution)/shard_map/ppermute | solution.py:825
  90.9 2.9 %collective-permute-done.8 = bf16[2,128,128]{2,1,0:T(8,128)(2,1)S(1)} collective-permute-done((bf16[2,128,128]{2,1,0:T(8,128)(2,1)S(1)}, bf16[2,128,128]{2,1,0:T(8,128)(2,1)S(1)}, u32[]{:S(2)}, u32[]{:S(2)}) %collective-permute-start.8) | collective-permute-done | bytes 65568 | tf_op jit(solution)/shard_map/ppermute | solution.py:825
  93.8 6.9 %collective-permute-done.7 = bf16[2,128,128]{2,1,0:T(8,128)(2,1)S(1)} collective-permute-done((bf16[2,128,128]{2,1,0:T(8,128)(2,1)S(1)}, bf16[2,128,128]{2,1,0:T(8,128)(2,1)S(1)}, u32[]{:S(2)}, u32[]{:S(2)}) %collective-permute-start.7) | collective-permute-done | bytes 65568 | tf_op jit(solution)/shard_map/ppermute | solution.py:825
  100.8 0.5 collective-permute-done.11.refs_4_
  101.3 1.1 %collective-permute-done.12.refs_5_ = bf16[400,512]{1,0:T(8,128)(2,1)S(1)} collective-permute-done((bf16[400,512]{1,0:T(8,128)(2,1)}, bf16[400,512]{1,0:T(8,128)(2,1)S(1)}, u32[]{:S(2)}, u32[]{:S(2)}) %collective-permute-start.12) | collective-permute-done | bytes 409632 | tf_op jit(solution)/shard_map/ppermute | solution.py:815
  102.4 0.5 collective-permute-start.15
  102.9 2.5 %collective-permute-start.14 = (bf16[64,128]{1,0:T(8,128)(2,1)S(1)}, bf16[64,128]{1,0:T(8,128)(2,1)S(1)}, u32[]{:S(2)}, u32[]{:S(2)}) collective-permute-start(bf16[64,128]{1,0:T(8,128)(2,1)S(1)} %get-tuple-element.64), channel_id=1, source_target_pairs={{0,2},{1,3},{2,0},{3,1},{4,6},{5,7},{6,4},{7,5},{8,10},{9,11},{10,... | collective-permute-start | bytes 49160 | tf_op jit(solution)/shard_map/ppermute | solution.py:825
  105.3 1.2 %collective-permute-start.13 = (bf16[64,128]{1,0:T(8,128)(2,1)S(1)}, bf16[64,128]{1,0:T(8,128)(2,1)S(1)}, u32[]{:S(2)}, u32[]{:S(2)}) collective-permute-start(bf16[64,128]{1,0:T(8,128)(2,1)S(1)} %get-tuple-element.62), channel_id=1, source_target_pairs={{0,16},{1,17},{2,18},{3,19},{4,20},{5,21},{6,22},{7,23},{8,24},{9,... | collective-permute-start | bytes 49160 | tf_op jit(solution)/shard_map/ppermute | solution.py:825
  106.6 3.6 %shard_map.187 = (bf16[576,512]{1,0:T(8,128)(2,1)}, bf16[72,2,1024]{2,1,0:T(2,128)(2,1)}) custom-call(s32[8,384]{1,0:T(8,128)} %constant.107.clone.refs_4_.refs_0_, s32[16,128]{1,0:T(8,128)} %constant.108.clone.refs_5_.refs_1_, bf16[400,512]{1,0:T(8,128)(2,1)} %get-tuple-element.40.refs_2_, bf16[400,512]{1,0:T(8,128)(2,1)} %copy-done, ...), custom_call_target="tpu_custom_call" | custom-call | tf_op jit(solution)/shard_map/pallas_call | solution.py:241
  110.2 0.6 fusion.8
  (25 shorter events, 0.5 us)
Async XLA Ops:
  4.7 14.2 %collective-permute-start = (bf16[400,512]{1,0:T(8,128)(2,1)}, bf16[400,512]{1,0:T(8,128)(2,1)S(1)}, u32[]{:S(2)}, u32[]{:S(2)}) collective-permute-start(bf16[400,512]{1,0:T(8,128)(2,1)} %get-tuple-element.30), channel_id=1, source_target_pairs={{16,0},{17,1},{18,2},{19,3},{20,4},{21,5},{22,6},{23,7},{24,8},{25... | collective-permute-start | bytes 1228808 | tf_op jit(solution)/shard_map/ppermute | solution.py:815
  8.7 16.5 %collective-permute-start.1 = (bf16[400,512]{1,0:T(8,128)(2,1)}, bf16[400,512]{1,0:T(8,128)(2,1)S(1)}, u32[]{:S(2)}, u32[]{:S(2)}) collective-permute-start(bf16[400,512]{1,0:T(8,128)(2,1)} %get-tuple-element.31), channel_id=1, source_target_pairs={{1,0},{2,1},{3,2},{4,3},{5,4},{6,5},{7,6},{8,7},{9,8},{10,9},{11,1... | collective-permute-start | bytes 1228808 | tf_op jit(solution)/shard_map/ppermute | solution.py:815
  14.2 12.3 %collective-permute-start.2 = (bf16[400,512]{1,0:T(8,128)(2,1)}, bf16[400,512]{1,0:T(8,128)(2,1)S(1)}, u32[]{:S(2)}, u32[]{:S(2)}) collective-permute-start(bf16[400,512]{1,0:T(8,128)(2,1)} %get-tuple-element.32), channel_id=1, source_target_pairs={{17,0},{18,1},{19,2},{20,3},{21,4},{22,5},{23,6},{24,7},{25,8},{26... | collective-permute-start | bytes 1228808 | tf_op jit(solution)/shard_map/ppermute | solution.py:815
  18.9 7.6 %copy-start.3 = (bf16[400,512]{1,0:T(8,128)(2,1)}, bf16[400,512]{1,0:T(8,128)(2,1)S(1)}, u32[]{:S(2)}) copy-start(bf16[400,512]{1,0:T(8,128)(2,1)S(1)} %collective-permute-done.q1_ref) | copy-start | bytes 1228804
  25.2 1.4 %copy-start.4 = (bf16[400,512]{1,0:T(8,128)(2,1)}, bf16[400,512]{1,0:T(8,128)(2,1)S(1)}, u32[]{:S(2)}) copy-start(bf16[400,512]{1,0:T(8,128)(2,1)S(1)} %collective-permute-done.1.q2_ref) | copy-start | bytes 1228804
  26.5 0.8 copy-start.5
  60.9 4.4 %collective-permute-start.3 = (bf16[4,8,128,128]{3,2,1,0:T(8,128)(2,1)}, bf16[4,8,128,128]{3,2,1,0:T(8,128)(2,1)S(1)}, u32[]{:S(2)}, u32[]{:S(2)}) collective-permute-start(bf16[4,8,128,128]{3,2,1,0:T(8,128)(2,1)} %get-tuple-element.34), channel_id=1, source_target_pairs={{0,1},{1,0},{2,3},{3,2},{4,5},{5,4},{6,7},{7,6},{8,9},{9,8},{10,11... | collective-permute-start | bytes 3145736 | tf_op jit(solution)/shard_map/ppermute | solution.py:825
  66.8 15.8 %collective-permute-start.6 = (bf16[8,128,128]{2,1,0:T(8,128)(2,1)S(1)}, bf16[8,128,128]{2,1,0:T(8,128)(2,1)S(1)}, u32[]{:S(2)}, u32[]{:S(2)}) collective-permute-start(bf16[8,128,128]{2,1,0:T(8,128)(2,1)S(1)} %get-tuple-element.44), channel_id=1, source_target_pairs={{0,96},{1,97},{2,98},{3,99},{4,100},{5,101},{6,102},{7,103},{8,104... | collective-permute-start | bytes 786440 | tf_op jit(solution)/shard_map/ppermute | solution.py:825
  70.2 13.2 %collective-permute-start.5 = (bf16[8,128,128]{2,1,0:T(8,128)(2,1)S(1)}, bf16[8,128,128]{2,1,0:T(8,128)(2,1)S(1)}, u32[]{:S(2)}, u32[]{:S(2)}) collective-permute-start(bf16[8,128,128]{2,1,0:T(8,128)(2,1)S(1)} %get-tuple-element.43), channel_id=1, source_target_pairs={{0,64},{1,65},{2,66},{3,67},{4,68},{5,69},{6,70},{7,71},{8,72},{9,... | collective-permute-start | bytes 786440 | tf_op jit(solution)/shard_map/ppermute | solution.py:825
  70.5 12.9 %collective-permute-start.4 = (bf16[8,128,128]{2,1,0:T(8,128)(2,1)S(1)}, bf16[8,128,128]{2,1,0:T(8,128)(2,1)S(1)}, u32[]{:S(2)}, u32[]{:S(2)}) collective-permute-start(bf16[8,128,128]{2,1,0:T(8,128)(2,1)S(1)} %get-tuple-element.42), channel_id=1, source_target_pairs={{0,32},{1,33},{2,34},{3,35},{4,36},{5,37},{6,38},{7,39},{8,40},{9,... | collective-permute-start | bytes 786440 | tf_op jit(solution)/shard_map/ppermute | solution.py:825
  79.0 21.8 %collective-permute-start.10 = (bf16[400,512]{1,0:T(8,128)(2,1)}, bf16[400,512]{1,0:T(8,128)(2,1)S(1)}, u32[]{:S(2)}, u32[]{:S(2)}) collective-permute-start(bf16[400,512]{1,0:T(8,128)(2,1)} %get-tuple-element.45), channel_id=1, source_target_pairs={{112,0},{113,1},{114,2},{115,3},{116,4},{117,5},{118,6},{119,7},{1... | collective-permute-start | bytes 1228808 | tf_op jit(solution)/shard_map/ppermute | solution.py:815
  79.8 21.5 %collective-permute-start.11 = (bf16[400,512]{1,0:T(8,128)(2,1)}, bf16[400,512]{1,0:T(8,128)(2,1)S(1)}, u32[]{:S(2)}, u32[]{:S(2)}) collective-permute-start(bf16[400,512]{1,0:T(8,128)(2,1)} %get-tuple-element.46), channel_id=1, source_target_pairs={{15,0},{0,1},{1,2},{2,3},{3,4},{4,5},{5,6},{6,7},{7,8},{8,9},{9,10... | collective-permute-start | bytes 1228808 | tf_op jit(solution)/shard_map/ppermute | solution.py:815
  82.6 19.7 %collective-permute-start.12 = (bf16[400,512]{1,0:T(8,128)(2,1)}, bf16[400,512]{1,0:T(8,128)(2,1)S(1)}, u32[]{:S(2)}, u32[]{:S(2)}) collective-permute-start(bf16[400,512]{1,0:T(8,128)(2,1)} %get-tuple-element.47), channel_id=1, source_target_pairs={{127,0},{112,1},{113,2},{114,3},{115,4},{116,5},{117,6},{118,7},{1... | collective-permute-start | bytes 1228808 | tf_op jit(solution)/shard_map/ppermute | solution.py:815
  83.6 7.3 %collective-permute-start.9 = (bf16[2,128,128]{2,1,0:T(8,128)(2,1)S(1)}, bf16[2,128,128]{2,1,0:T(8,128)(2,1)S(1)}, u32[]{:S(2)}, u32[]{:S(2)}) collective-permute-start(bf16[2,128,128]{2,1,0:T(8,128)(2,1)S(1)} %get-tuple-element.60), channel_id=1, source_target_pairs={{0,12},{1,13},{2,14},{3,15},{4,8},{5,9},{6,10},{7,11},{8,4},{9,5},... | collective-permute-start | bytes 196616 | tf_op jit(solution)/shard_map/ppermute | solution.py:825
  87.7 6.1 %collective-permute-start.8 = (bf16[2,128,128]{2,1,0:T(8,128)(2,1)S(1)}, bf16[2,128,128]{2,1,0:T(8,128)(2,1)S(1)}, u32[]{:S(2)}, u32[]{:S(2)}) collective-permute-start(bf16[2,128,128]{2,1,0:T(8,128)(2,1)S(1)} %get-tuple-element.61), channel_id=1, source_target_pairs={{0,8},{1,9},{2,10},{3,11},{4,12},{5,13},{6,14},{7,15},{8,0},{9,1},... | collective-permute-start | bytes 196616 | tf_op jit(solution)/shard_map/ppermute | solution.py:825
  90.9 9.9 %collective-permute-start.7 = (bf16[2,128,128]{2,1,0:T(8,128)(2,1)S(1)}, bf16[2,128,128]{2,1,0:T(8,128)(2,1)S(1)}, u32[]{:S(2)}, u32[]{:S(2)}) collective-permute-start(bf16[2,128,128]{2,1,0:T(8,128)(2,1)S(1)} %get-tuple-element.59), channel_id=1, source_target_pairs={{0,4},{1,5},{2,6},{3,7},{4,0},{5,1},{6,2},{7,3},{8,12},{9,13},{10,... | collective-permute-start | bytes 196616 | tf_op jit(solution)/shard_map/ppermute | solution.py:825
  100.8 5.8 %copy-start = (bf16[400,512]{1,0:T(8,128)(2,1)}, bf16[400,512]{1,0:T(8,128)(2,1)S(1)}, u32[]{:S(2)}) copy-start(bf16[400,512]{1,0:T(8,128)(2,1)S(1)} %collective-permute-done.10.refs_3_) | copy-start | bytes 1228804
  101.3 5.3 %copy-start.1 = (bf16[400,512]{1,0:T(8,128)(2,1)}, bf16[400,512]{1,0:T(8,128)(2,1)S(1)}, u32[]{:S(2)}) copy-start(bf16[400,512]{1,0:T(8,128)(2,1)S(1)} %collective-permute-done.11.refs_4_) | copy-start | bytes 1228804
  102.4 4.2 %copy-start.2 = (bf16[400,512]{1,0:T(8,128)(2,1)}, bf16[400,512]{1,0:T(8,128)(2,1)S(1)}, u32[]{:S(2)}) copy-start(bf16[400,512]{1,0:T(8,128)(2,1)S(1)} %collective-permute-done.12.refs_5_) | copy-start | bytes 1228804
  102.4 7.8 %collective-permute-start.15 = (bf16[64,128]{1,0:T(8,128)(2,1)S(1)}, bf16[64,128]{1,0:T(8,128)(2,1)S(1)}, u32[]{:S(2)}, u32[]{:S(2)}) collective-permute-start(bf16[64,128]{1,0:T(8,128)(2,1)S(1)} %get-tuple-element.63), channel_id=1, source_target_pairs={{0,18},{1,19},{2,16},{3,17},{4,22},{5,23},{6,20},{7,21},{8,26},{9,... | collective-permute-start | bytes 49160 | tf_op jit(solution)/shard_map/ppermute | solution.py:825
  102.9 7.3 %collective-permute-start.14 = (bf16[64,128]{1,0:T(8,128)(2,1)S(1)}, bf16[64,128]{1,0:T(8,128)(2,1)S(1)}, u32[]{:S(2)}, u32[]{:S(2)}) collective-permute-start(bf16[64,128]{1,0:T(8,128)(2,1)S(1)} %get-tuple-element.64), channel_id=1, source_target_pairs={{0,2},{1,3},{2,0},{3,1},{4,6},{5,7},{6,4},{7,5},{8,10},{9,11},{10,... | collective-permute-start | bytes 49160 | tf_op jit(solution)/shard_map/ppermute | solution.py:825
  105.3 4.8 %collective-permute-start.13 = (bf16[64,128]{1,0:T(8,128)(2,1)S(1)}, bf16[64,128]{1,0:T(8,128)(2,1)S(1)}, u32[]{:S(2)}, u32[]{:S(2)}) collective-permute-start(bf16[64,128]{1,0:T(8,128)(2,1)S(1)} %get-tuple-element.62), channel_id=1, source_target_pairs={{0,16},{1,17},{2,18},{3,19},{4,20},{5,21},{6,22},{7,23},{8,24},{9,... | collective-permute-start | bytes 49160 | tf_op jit(solution)/shard_map/ppermute | solution.py:825
